TPU v7x, 256 devices: a whole 4x4x8 slice. The times are simulated.
256 devices in a mesh: row: 64 (over y, z, core), grp: 4 (over x).
Axes of the slice: x: 4, y: 4, z: 8, core: 2. Of those that a mesh axis runs over, the one named last changes fastest.
Arguments:
- snapshots: float32 [256, 1048576], P('row', 'grp'), may hold values from -75 to 75, as said below
- lumped_mass: float32 [4, 262144], P('grp', 'row'), may hold values from 0.1 to 10
Outputs:
- pod_modes: float32 [256, 4, 262144], P(None, 'grp', 'row')
- triangle: float32 [256, 256], replicated
Inputs may be any that keep to these rules, and one draw needn't show every extreme that they name: Real values; the snapshots have full rank.
All inputs are finite; a program needn't handle non-finite values.
Results may differ from a plain program's by a relative error of at most 0.0001.
Values sent between devices are 32-bit elements; how exact they have to be, the bound alone decides.
A program may use at most 128 MiB of HBM per device.

v0:
```python
import jax
import jax.numpy as jnp
from jax import lax
from jax.sharding import PartitionSpec as P


def body(snapshots, lumped_mass):
    received = lax.all_to_all(snapshots, "row", split_axis=1, concat_axis=0, tiled=True)
    width = received.shape[0]
    rows_here = received.shape[1]
    row_count = rows_here * lax.axis_size("row") * lax.axis_size("grp")
    weighted = received * jnp.sqrt(lumped_mass)
    own_gram = (
        lax.dot_general(
            weighted, weighted, (((1,), (1,)), ((), ())), precision=lax.Precision.HIGHEST
        )
        / row_count
    )
    full_gram = lax.psum(own_gram, ("row", "grp"))
    factor_low = jnp.linalg.cholesky(full_gram)
    projected = jax.scipy.linalg.solve_triangular(factor_low, weighted, lower=True)
    return (projected.reshape(width, 1, rows_here), jnp.transpose(factor_low))


def solution(mesh):
    return jax.shard_map(
        body,
        mesh=mesh,
        in_specs=(P("row", "grp"), P("grp", "row")),
        out_specs=(P(None, "grp", "row"), P()),
        check_vma=False,
    )
```

profile of v0, /device:TPU:1, one launch (start us, length us, event | category | flops | bytes accessed | tf_op | source)
XLA Modules:
  0.0 464.7 jit_solution(6829169133406444380)
XLA Ops:
  7.2 13.4 %all-to-all-start = ((f32[4,64,4096]{2,0,1:T(4,128)}), f32[4,64,4096]{2,0,1:T(4,128)}, u32[]{:S(2)}, u32[]{:S(2)}) async-start(f32[4,64,4096]{2,0,1:T(4,128)} %bitcast.41), calls=%async_computation | async-start | bytes 8388608 | tf_op jit(solution)/shard_map/all_to_all | solution.py:8
  20.7 95.8 %all-to-all-done = f32[4,64,4096]{2,0,1:T(4,128)} async-done(((f32[4,64,4096]{2,0,1:T(4,128)}), f32[4,64,4096]{2,0,1:T(4,128)}, u32[]{:S(2)}, u32[]{:S(2)}) %all-to-all-start) | async-done | bytes 4194336 | tf_op jit(solution)/shard_map/all_to_all | solution.py:8
  116.4 5.7 %broadcast_multiply_fusion.1 = f32[64,4,4096]{2,1,0:T(4,128)} fusion(f32[4096]{0:T(1024)S(1)} %bitcast.42, f32[4,64,4096]{2,0,1:T(4,128)} %all-to-all-done), kind=kLoop, calls=%fused_computation.7 | loop fusion | flops 1048576 | bytes 8404992 | tf_op jit(solution)/shard_map/mul | solution.py:12
  122.2 5.3 %mul.21 = f32[256,4096]{1,0:T(8,128)} reshape(f32[64,4,4096]{2,1,0:T(4,128)} %broadcast_multiply_fusion.1) | data formatting | bytes 8388608 | tf_op jit(solution)/shard_map/mul | solution.py:12
  127.4 7.7 %convolution_multiply_fusion = f32[256,256]{0,1:T(8,128)} fusion(f32[256,4096]{1,0:T(8,128)} %mul.21), kind=kOutput, calls=%fused_computation.8 | convolution fusion | flops 3221291008 | bytes 4456448 | tf_op jit(solution)/shard_map/dot_general | solution.py:14
  135.2 5.3 %all_to_all.17 = f32[256,4096]{1,0:T(8,128)} reshape(f32[64,4,4096]{2,1,0:T(4,128)} %bitcast.1) | data formatting | bytes 8388608 | tf_op jit(solution)/shard_map/all_to_all | solution.py:8
  140.4 4.8 %broadcast_multiply_fusion = f32[256,4096]{1,0:T(8,128)} fusion(f32[256,4096]{1,0:T(8,128)} %all_to_all.17, f32[4096]{0:T(1024)S(1)} %bitcast.43), kind=kLoop, calls=%fused_computation.6 | loop fusion | flops 1048576 | bytes 8404992 | tf_op jit(solution)/shard_map/mul | solution.py:12
  145.2 235.4 %all-reduce.3.cloned.1.call-done = f32[256,256]{0,1:T(8,128)} async-done(((f32[256,256]{0,1:T(8,128)}), f32[256,256]{0,1:T(8,128)}) %all-reduce.3.cloned.1.call-update) | async-done | bytes 262160 | tf_op jit(solution)/shard_map/psum | solution.py:19
  380.6 1.1 copy.10
  381.7 1.0 fusion.2
  382.7 11.7 %cholesky.50 = f32[128,128]{1,0:T(8,128)S(1)} custom-call(f32[128,128]{1,0:T(8,128)S(1)} %cholesky.118), custom_call_target="Cholesky" | custom-call | tf_op jit(solution)/shard_map/jit(cholesky)/cholesky | solution.py:20
  394.5 9.8 %custom-call.15 = f32[1,128,128]{1,2,0:T(8,128)S(1)} custom-call(f32[1,128,128]{2,1,0:T(8,128)S(1)} %get-tuple-element.29), custom_call_target="InvertDiagBlocksLowerTriangular" | custom-call | tf_op jit(solution)/shard_map/jit(cholesky)/cholesky | solution.py:20
  404.8 11.7 %cholesky.105 = f32[128,128]{1,0:T(8,128)S(1)} custom-call(f32[128,128]{1,0:T(8,128)S(1)} %convolution_subtract_fusion.1), custom_call_target="Cholesky" | custom-call | tf_op jit(solution)/shard_map/jit(cholesky)/cholesky | solution.py:20
  416.6 0.7 compare_reduce_fusion
  418.7 4.1 while.1
  418.7 0.6 fusion.18
  419.3 1.4 bitcast_dynamic-update-slice_fusion.2
  421.4 1.4 bitcast_dynamic-update-slice_fusion.2
  422.8 19.9 %custom-call.16 = f32[2,128,128]{1,2,0:T(8,128)S(1)} custom-call(f32[2,128,128]{2,1,0:T(8,128)S(1)} %get-tuple-element.9), custom_call_target="InvertDiagBlocksLowerTriangular" | custom-call | tf_op jit(solution)/shard_map/jit(_solve_triangular)/triangular_solve | solution.py:21
  442.8 3.6 fusion
  446.4 1.9 convolution_subtract_fusion
  448.3 1.9 fusion.6
  450.7 6.3 %copy.11 = f32[256,1,4096]{2,1,0:T(1,128)} copy(f32[256,1,4096]{2,0,1:T(8,128)S(1)} %maximum_bitcast_fusion) | data formatting | bytes 8388608
  457.1 0.8 copy.12
  (21 shorter events, 1.8 us)
Async XLA Ops:
  7.2 13.4 %copy-start.1 = (f32[1,4096]{1,0:T(1,128)S(1)}, f32[1,4096]{1,0:T(1,128)}, u32[]{:S(2)}) copy-start(f32[1,4096]{1,0:T(1,128)} %param.3) | copy-start | bytes 49156
  7.2 109.2 %all-to-all-start = ((f32[4,64,4096]{2,0,1:T(4,128)}), f32[4,64,4096]{2,0,1:T(4,128)}, u32[]{:S(2)}, u32[]{:S(2)}) async-start(f32[4,64,4096]{2,0,1:T(4,128)} %bitcast.41), calls=%async_computation | async-start | bytes 8388608 | tf_op jit(solution)/shard_map/all_to_all | solution.py:8
  20.5 360.1 %all-reduce.3.cloned.1.call-start = ((), (), s32[]{:S(2)}) async-start(), calls=%async_computation.1 | async-start | bytes 524288 | tf_op jit(solution)/shard_map/psum | solution.py:19
  442.7 3.7 copy-start
Sparse Core Ops, SparseCore 0:
  135.3 245.3 all-reduce.2
where the time goes:
time: 466 us; the launch traced here: 465 us
  waiting for transfers between devices  331 us (71%)
  other arithmetic  65.9 us (14%)
  local copies, waits for them, and re-layouts  23 us (5%)
  matrix products  15.7 us (3%)
  between operations  15.5 us (3%)
  starting transfers between devices  13.4 us (3%)
    psum x1, waiting for transfers between devices, body(): full_gram = lax.psum(own_gram, ('row', 'grp'))  235 us
    all_to_all x1, waiting for transfers between devices, body(): lax.all_to_all(snapshots, 'row', split_axis=1, concat_axis=0, tiled=True)  95.8 us
    another operation x6, other arithmetic, body(): factor_low = jnp.linalg.cholesky(full_gram)  34 us
    another operation x2, other arithmetic, body(): jax.scipy.linalg.solve_triangular(factor_low, weighted, lower=True)  19.9 us
    all_to_all x1, starting transfers between devices, body(): lax.all_to_all(snapshots, 'row', split_axis=1, concat_axis=0, tiled=True)  13.4 us
    mul x2, other arithmetic, body(): weighted = received * jnp.sqrt(lumped_mass)  10.5 us
  transfers between devices with their start and end apart: 2, of which 2 were waited for; matrix products, arithmetic and copies ran while one was open for 1% of the time, Pallas kernels for 0%

commit v1 on v0

v1 whole, which is shorter than its diff:
```python
import jax
import jax.numpy as jnp
from jax import lax
from jax.experimental import pallas as pl
from jax.experimental.pallas import tpu as pltpu
from jax.sharding import PartitionSpec as P

MESH = pl.DeviceIdType.MESH
F32 = jnp.float32
BF16 = jnp.bfloat16
K = 256
COORDS = 4096
TILES = 32
CHUNKS = 4
CT = TILES // CHUNKS
NT = (((1,), (1,)), ((), ()))
NN = (((1,), (0,)), ((), ()))


def split3(v):
    h = v.astype(BF16)
    r = v - h.astype(F32)
    m = r.astype(BF16)
    l = (r - m.astype(F32)).astype(BF16)
    return h, m, l


def gather_kernel(x_ref, w_ref, xs_ref, g_ref, buf, xs, gs, gx, half, parts, zp,
                  own_sem, in_send, in_recv, out_sem, red_send, red_recv):
    r = lax.axis_index("row")
    g = lax.axis_index("grp")
    y, z, c = r // 16, (r // 2) % 8, r % 2

    def dev(x_, y_, z_, c_):
        return (y_ * 16 + z_ * 2 + c_, x_)

    barrier = pltpu.get_barrier_semaphore()

    @pl.loop(1, 64)
    def _(o):
        pl.semaphore_signal(barrier, 1, device_id=(lax.rem(r + o, 64), g), device_id_type=MESH)

    for dx in range(1, 4):
        for dy in range(4):
            pl.semaphore_signal(barrier, 1, device_id=dev(lax.rem(g + dx, 4), lax.rem(y + dy, 4), z, c), device_id_type=MESH)
    pl.semaphore_wait(barrier, 63 + 12)

    rows = 128 // CHUNKS
    for ch in range(CHUNKS):
        @pl.loop(1, 64)
        def _(o):
            d = lax.rem(r + o, 64)
            pltpu.make_async_remote_copy(
                src_ref=x_ref.at[pl.ds(pl.multiple_of(d * 128 + ch * rows, rows), rows)],
                dst_ref=buf.at[r, pl.ds(ch * rows, rows)],
                send_sem=in_send, recv_sem=in_recv.at[ch],
                device_id=(d, g), device_id_type=MESH).start()
    own = pltpu.make_async_copy(x_ref.at[pl.ds(pl.multiple_of(r * 128, 128), 128)], buf.at[r], own_sem)
    own.start()
    own.wait()
    gs[...] = jnp.zeros_like(gs)
    gx[...] = jnp.zeros_like(gx)
    low = lax.broadcasted_iota(jnp.int32, (32, 8, 128), 1) < 4

    for ch in range(CHUNKS):
        arrived = buf.at[pl.ds(0, 63), pl.ds(0, rows)]
        pltpu.make_async_copy(arrived, arrived, in_recv.at[ch]).wait()

        @pl.loop(0, CT // 2)
        def _(q):
            pair = ch * (CT // 2) + q
            v = buf[:, pl.ds(pl.multiple_of(pair * 8, 8), 8), :].reshape(32, 2, 8, 128)
            even, odd = v[:, 0], v[:, 1]
            first = jnp.where(low, even, pltpu.roll(odd, 4, 1)).reshape(K, 128)
            second = jnp.where(low, pltpu.roll(even, 4, 1), odd).reshape(K, 128)
            sw = jnp.sqrt(w_ref[:, pl.ds(pl.multiple_of(pair * 256, 256), 256)])
            wide = jnp.concatenate([first, second], axis=1) * sw
            h, m, l = split3(wide)
            cols = pl.ds(pl.multiple_of(pair * 256, 256), 256)
            xs[0, :, cols] = h
            xs[1, :, cols] = m
            xs[2, :, cols] = l
            gs[...] += lax.dot_general(h, h, NT, preferred_element_type=F32) + lax.dot_general(m, m, NT, preferred_element_type=F32)
            gx[...] += lax.dot_general(h, m, NT, preferred_element_type=F32) + lax.dot_general(h, l, NT, preferred_element_type=F32)

        cols = pl.ds(ch * (COORDS // CHUNKS), COORDS // CHUNKS)
        pltpu.make_async_copy(xs.at[:, :, cols], xs_ref.at[:, :, cols], out_sem.at[ch]).start()

    cross = gx[...]
    gs[...] = (gs[...] + (cross + cross.T)) * (1.0 / (COORDS * 256))

    def send(src, dst, i, to):
        pltpu.make_async_remote_copy(src_ref=src, dst_ref=dst, send_sem=red_send.at[i], recv_sem=red_recv.at[i],
                                     device_id=to, device_id_type=MESH).start()

    def wait(ref, sem):
        pltpu.make_async_copy(ref, ref, sem).wait()

    partner = dev(g, y, z, 1 - c)
    send(gs.at[pl.ds(pl.multiple_of((1 - c) * 128, 128), 128)], half, 0, partner)
    wait(half, red_recv.at[0])
    half[...] += gs[pl.ds(pl.multiple_of(c * 128, 128), 128)]
    peers = [(dx, dy) for dx in range(4) for dy in range(4) if (dx, dy) != (0, 0)]
    peers.sort(key=lambda p: -(min(p[0], 4 - p[0]) + min(p[1], 4 - p[1])))
    for dx, dy in peers:
        px, py = lax.rem(g + dx, 4), lax.rem(y + dy, 4)
        send(half.at[pl.ds(pl.multiple_of((px * 4 + py) * 8, 8), 8)], parts.at[dx * 4 + dy - 1], 1, dev(px, py, z, c))
    wait(parts, red_recv.at[1])
    mine = half[pl.ds(pl.multiple_of((g * 4 + y) * 8, 8), 8)]
    for i in range(15):
        mine = mine + parts[i]
    zp[z] = mine
    for dz in (4, 3, 5, 2, 6, 1, 7):
        send(zp.at[z], zp.at[z], 2, dev(g, y, lax.rem(z + dz, 8), c))
    wait(zp.at[pl.ds(0, 7)], red_recv.at[2])
    total = zp[0]
    for i in range(1, 8):
        total = total + zp[i]
    here = pl.ds(pl.multiple_of(c * 128 + (g * 4 + y) * 8, 8), 8)
    g_ref[here] = total
    for dx, dy in peers:
        send(g_ref.at[here], g_ref.at[here], 3, dev(lax.rem(g + dx, 4), lax.rem(y + dy, 4), z, c))
    wait(g_ref.at[pl.ds(0, 120)], red_recv.at[3])
    there = pl.ds(pl.multiple_of(c * 128, 128), 128)
    send(g_ref.at[there], g_ref.at[there], 4, partner)
    wait(half, red_recv.at[4])

    wait(half, red_send.at[0])
    wait(parts, red_send.at[1])
    wait(zp.at[pl.ds(0, 7)], red_send.at[2])
    wait(g_ref.at[pl.ds(0, 120)], red_send.at[3])
    wait(half, red_send.at[4])
    wait(buf.at[pl.ds(0, 63)], in_send)
    for ch in range(CHUNKS):
        cols = pl.ds(ch * (COORDS // CHUNKS), COORDS // CHUNKS)
        pltpu.make_async_copy(xs.at[:, :, cols], xs_ref.at[:, :, cols], out_sem.at[ch]).wait()


B = 64
NB = K // B
STEP = 4


def eliminate(block):
    rows = lax.broadcasted_iota(jnp.int32, (B, 2 * B), 0)
    lanes = lax.broadcasted_iota(jnp.int32, (B, 2 * B), 1)
    m = jnp.concatenate([block, jnp.where(rows == lanes, 1.0, 0.0)[:, :B]], axis=1)
    tiles = [m[8 * t:8 * t + 8] for t in range(B // 8)]
    done = []
    full = (8, 2 * B)
    for j in range(0, B, STEP):
        t0, s0 = j // 8, j % 8
        top = tiles[t0]
        row = [jnp.broadcast_to(top[s0 + a:s0 + a + 1, :], full) for a in range(STEP)]
        d = {(a, b): jnp.broadcast_to(top[s0 + a:s0 + a + 1, j + b:j + b + 1], full) for a in range(STEP) for b in range(a + 1)}
        col = {(t, a): jnp.broadcast_to(tiles[t][:, j + a:j + a + 1], full) for t in range(t0, B // 8) for a in range(STEP)}
        inv = []
        for a in range(STEP):
            inv.append(1.0 / d[a, a])
            root = lax.rsqrt(d[a, a])
            root = root * (1.5 - 0.5 * d[a, a] * root * root)
            done.append((row[a] * root)[0:1])
            for b in range(a + 1, STEP):
                f = d[b, a] * inv[a]
                for k in range(b, STEP):
                    d[k, b] = d[k, b] - d[k, a] * f
                row[b] = row[b] - row[a] * f
                for t in range(t0, B // 8):
                    col[t, b] = col[t, b] - col[t, a] * f
        scaled = [row[a] * inv[a] for a in range(STEP)]
        for t in range(t0, B // 8):
            if 8 * t + 7 < j + STEP:
                continue
            for a in range(STEP):
                tiles[t] = tiles[t] - col[t, a] * scaled[a]
    return jnp.concatenate(done, axis=0)[:, B:]


def dot(a, b, dims):
    return lax.dot_general(a, b, dims, precision=lax.Precision.HIGHEST, preferred_element_type=F32)


def factor_kernel(g_ref, xs_ref, out_ref, tri_ref, a_ref, p_ref, xs, ob, in_sem, out_sem):
    pieces = 4
    wide = COORDS // pieces
    for i in range(pieces):
        cols = pl.ds(i * wide, wide)
        pltpu.make_async_copy(xs_ref.at[:, :, cols], xs.at[:, :, cols], in_sem.at[i]).start()
    a_ref[...] = g_ref[...]
    rows = lax.broadcasted_iota(jnp.int32, (K, K), 0)
    lanes = lax.broadcasted_iota(jnp.int32, (K, K), 1)
    p_ref[...] = jnp.where(rows == lanes, 1.0, 0.0)
    for j in range(NB):
        lo, hi = j * B, j * B + B
        inv = eliminate(a_ref[lo:hi, lo:hi])
        top_a = dot(inv, a_ref[lo:hi, :], NN)
        top_p = dot(inv, p_ref[lo:hi, :], NN)
        if j + 1 < NB:
            side = dot(a_ref[hi:, lo:hi], inv, NT)
            a_ref[hi:, :] -= dot(side, top_a, NN)
            p_ref[hi:, :] -= dot(side, top_p, NN)
        a_ref[lo:hi, :] = top_a
        p_ref[lo:hi, :] = top_p
    tri_ref[...] = jnp.where(lanes >= rows, a_ref[...], 0.0)
    wh, wm, wl = split3(p_ref[...])

    def mm(a, b):
        return lax.dot_general(a, b, NN, preferred_element_type=F32)

    for i in range(pieces):
        cols = pl.ds(i * wide, wide)
        pltpu.make_async_copy(xs_ref.at[:, :, cols], xs.at[:, :, cols], in_sem.at[i]).wait()

        @pl.loop(0, wide // 256)
        def _(q):
            n = i * (wide // 256) + q
            part = pl.ds(pl.multiple_of(n * 256, 256), 256)
            xh, xm, xl = xs[0, :, part], xs[1, :, part], xs[2, :, part]
            o = (mm(wh, xl) + mm(wl, xh) + mm(wm, xm)) + (mm(wh, xm) + mm(wm, xh)) + mm(wh, xh)
            ob[pl.ds(2 * n, K, stride=TILES), :] = o[:, :128]
            ob[pl.ds(2 * n + 1, K, stride=TILES), :] = o[:, 128:]

    copy = pltpu.make_async_copy(ob, out_ref, out_sem)
    copy.start()
    copy.wait()


def body(snapshots, lumped_mass):
    x = snapshots.reshape(4, 2048, 128).transpose(1, 0, 2).reshape(8192, 128)
    anywhere = pl.BlockSpec(memory_space=pl.ANY)
    hbm = pl.BlockSpec(memory_space=pltpu.HBM)
    vmem = pl.BlockSpec(memory_space=pltpu.VMEM)
    dma = pltpu.SemaphoreType.DMA
    xs, gram = pl.pallas_call(
        gather_kernel,
        name="gather_gram",
        out_shape=(jax.ShapeDtypeStruct((3, K, COORDS), BF16), jax.ShapeDtypeStruct((K, K), F32)),
        in_specs=[hbm, vmem],
        out_specs=(anywhere, vmem),
        scratch_shapes=[
            pltpu.VMEM((64, 128, 128), F32),
            pltpu.VMEM((3, K, COORDS), BF16),
            pltpu.VMEM((K, K), F32),
            pltpu.VMEM((K, K), F32),
            pltpu.VMEM((128, K), F32),
            pltpu.VMEM((15, 8, K), F32),
            pltpu.VMEM((8, 8, K), F32),
            dma, dma, dma((CHUNKS,)), dma((CHUNKS,)), dma((5,)), dma((5,)),
        ],
        compiler_params=pltpu.CompilerParams(collective_id=0, has_side_effects=True, vmem_limit_bytes=58 * 2**20),
    )(x, lumped_mass)
    out, tri = pl.pallas_call(
        factor_kernel,
        name="factor_project",
        out_shape=(jax.ShapeDtypeStruct((8192, 128), F32), jax.ShapeDtypeStruct((K, K), F32)),
        in_specs=[vmem, anywhere],
        out_specs=(anywhere, vmem),
        scratch_shapes=[
            pltpu.VMEM((K, K), F32),
            pltpu.VMEM((K, K), F32),
            pltpu.VMEM((3, K, COORDS), BF16),
            pltpu.VMEM((8192, 128), F32),
            dma((4,)), dma,
        ],
        compiler_params=pltpu.CompilerParams(vmem_limit_bytes=58 * 2**20),
    )(gram, xs)
    return out.reshape(K, 1, COORDS), tri


def solution(mesh):
    return jax.shard_map(
        body,
        mesh=mesh,
        in_specs=(P("row", "grp"), P("grp", "row")),
        out_specs=(P(None, "grp", "row"), P()),
        check_vma=False,
    )
```

time: 466 us -> 153 us (0.33)
  waiting for transfers between devices: 331 us -> 0 us
  Pallas kernels: 0 us -> 152 us
  other arithmetic: 65.9 us -> 0 us
  local copies, waits for them, and re-layouts: 23 us -> 0 us
  matrix products: 15.7 us -> 0 us
  between operations: 15.5 us -> 0.64 us
  starting transfers between devices: 13.4 us -> 0 us
    psum x1 -> x0, waiting for transfers between devices: 235 us -> none  [body(): full_gram = lax.psum(own_gram, ('row', 'grp'))]
    pallas_call x0 -> x2, Pallas kernels: none -> 152 us  [the longest x1 126 us: body(): pl.pallas_call(gather_kernel, name='gather_gram', out_shape=(jax.ShapeDty...]
    all_to_all x1 -> x0, waiting for transfers between devices: 95.8 us -> none  [body(): lax.all_to_all(snapshots, 'row', split_axis=1, concat_axis=0, tiled=True)]
    another operation x8 -> x0, other arithmetic: 53.9 us -> none  [the longest x6 34 us: body(): factor_low = jnp.linalg.cholesky(full_gram)]
    all_to_all x1 -> x0, starting transfers between devices: 13.4 us -> none  [body(): lax.all_to_all(snapshots, 'row', split_axis=1, concat_axis=0, tiled=True)]
    mul x2 -> x0, other arithmetic: 10.5 us -> none  [body(): weighted = received * jnp.sqrt(lumped_mass)]
    another operation x5 -> x0, matrix products: 7.98 us -> none  [the longest x3 7.51 us: body(): jax.scipy.linalg.solve_triangular(factor_low, weighted, lower=True)]
    dot_general x1 -> x0, matrix products: 7.69 us -> none  [body(): lax.dot_general(weighted, weighted, (((1,), (1,)), ((), ())), precision=l...]
  transfers between devices with their start and end apart: 2 -> 0, of which waited for: 2 -> 0; matrix products, arithmetic and copies ran while one was open for 1% -> 0% of each run, Pallas kernels for 0% -> 0%
where the time goes in v1:
time: 153 us
  Pallas kernels  152 us (99%)
    pallas_call x1, Pallas kernels, body(): pl.pallas_call(gather_kernel, name='gather_gram', out_shape=(jax.ShapeDty...  126 us
    pallas_call x1, Pallas kernels, body(): pl.pallas_call(factor_kernel, name='factor_project', out_shape=(jax.Shape...  26.4 us

profile of v1, /device:TPU:1, one launch (start us, length us, event | category | flops | bytes accessed | tf_op | source)
XLA Modules:
  0.0 152.7 jit_solution(17035807000105720714)
XLA Ops:
  0.6 125.7 %gather_gram.1 = (bf16[3,256,4096]{2,1,0:T(8,128)(2,1)}, f32[256,256]{1,0:T(8,128)}) custom-call(f32[8192,128]{1,0:T(8,128)} %bitcast.6, f32[1,4096]{1,0:T(1,128)} %w_ref.1), custom_call_target="tpu_custom_call" | custom-call | tf_op jit(solution)/shard_map/gather_gram/pallas_call | solution.py:234
  126.3 26.4 %factor_project.1 = (f32[8192,128]{1,0:T(8,128)}, f32[256,256]{1,0:T(8,128)}) custom-call(f32[256,256]{1,0:T(8,128)} %get-tuple-element.6.g_ref, bf16[3,256,4096]{2,1,0:T(8,128)(2,1)} %get-tuple-element.7.xs_ref), custom_call_target="tpu_custom_call" | custom-call | tf_op jit(solution)/shard_map/factor_project/pallas_call | solution.py:252

commit v2 on v0

v2 whole, which is shorter than its diff:
```python
import jax
import jax.numpy as jnp
from jax import lax
from jax.experimental import pallas as pl
from jax.experimental.pallas import tpu as pltpu
from jax.sharding import PartitionSpec as P

MESH = pl.DeviceIdType.MESH
F32 = jnp.float32
BF16 = jnp.bfloat16
K = 256
COORDS = 4096
TILES = 32
FILL = 3
HELD = 8
LAG = 5
B = 64
STEP = 8
SCALE = 1.0 / 1048576
NT = (((1,), (1,)), ((), ()))
NN = (((1,), (0,)), ((), ()))


def split3(v):
    h = v.astype(BF16)
    r = v - h.astype(F32)
    m = r.astype(BF16)
    l = (r - m.astype(F32)).astype(BF16)
    return h, m, l


def mm(a, b, dims):
    return lax.dot_general(a, b, dims, preferred_element_type=F32)


def dot(a, b, dims):
    return lax.dot_general(a, b, dims, precision=lax.Precision.HIGHEST, preferred_element_type=F32)


def eliminate(block):
    rows = lax.broadcasted_iota(jnp.int32, (B, B), 0)
    lanes = lax.broadcasted_iota(jnp.int32, (B, B), 1)
    m = jnp.concatenate([block, jnp.where(rows == lanes, 1.0, 0.0)], axis=1)
    tiles = [m[8 * t:8 * t + 8] for t in range(B // 8)]
    done = []
    full = (8, 2 * B)
    for j in range(0, B, STEP):
        t0, s0 = j // 8, j % 8
        top = tiles[t0]
        row = [jnp.broadcast_to(top[s0 + a:s0 + a + 1, :], full) for a in range(STEP)]
        d = {(a, b): jnp.broadcast_to(top[s0 + a:s0 + a + 1, j + b:j + b + 1], full) for a in range(STEP) for b in range(a + 1)}
        live = [t for t in range(t0, B // 8) if 8 * t + 7 >= j + STEP]
        col = {(t, a): jnp.broadcast_to(tiles[t][:, j + a:j + a + 1], full) for t in live for a in range(STEP)}
        inv = []
        for a in range(STEP):
            inv.append(1.0 / d[a, a])
            root = lax.rsqrt(d[a, a])
            root = root * (1.5 - 0.5 * d[a, a] * root * root)
            done.append((row[a] * root)[0:1])
            for b in range(a + 1, STEP):
                f = d[b, a] * inv[a]
                for k in range(b, STEP):
                    d[k, b] = d[k, b] - d[k, a] * f
                row[b] = row[b] - row[a] * f
                for t in live:
                    col[t, b] = col[t, b] - col[t, a] * f
        scaled = [row[a] * inv[a] for a in range(STEP)]
        for t in live:
            for a in range(STEP):
                tiles[t] = tiles[t] - col[t, a] * scaled[a]
    return jnp.concatenate(done, axis=0)


def keep_upper(t):
    rows = lax.broadcasted_iota(jnp.int32, t.shape, 0)
    lanes = lax.broadcasted_iota(jnp.int32, t.shape, 1)
    return jnp.where(lanes >= rows, t, 0.0)


def pod_kernel(x_ref, w_ref, out_ref, tri_ref, buf, stage, xs, gram, p_ref, tmp, pack, parts, zparts, res,
               y_send, y_recv, z_send, z_recv, red_send, red_recv):
    r = lax.axis_index("row")
    g = lax.axis_index("grp")
    y, zc = r // 16, lax.rem(r, 16)
    phase_of = jnp.where(y < 2, 0, y - 1)

    def dev(x_, y_, zc_):
        return (y_ * 16 + zc_, x_)

    plane = [(dx, dy) for dx in range(4) for dy in range(4) if (dx, dy) != (0, 0)]
    plane.sort(key=lambda p: -(min(p[0], 4 - p[0]) + min(p[1], 4 - p[1])))

    barrier = pltpu.get_barrier_semaphore()

    @pl.loop(1, 16)
    def _(o):
        pl.semaphore_signal(barrier, 1, device_id=dev(g, y, lax.rem(zc + o, 16)), device_id_type=MESH)

    for dx, dy in plane:
        pl.semaphore_signal(barrier, 1, device_id=dev(lax.rem(g + dx, 4), lax.rem(y + dy, 4), zc), device_id_type=MESH)
    pl.semaphore_wait(barrier, 30)

    def block(plane_y, b):
        return x_ref.at[pl.ds(pl.multiple_of((plane_y * 16 + b) * 128, 128), 128)]

    def target(i):
        return lax.rem(zc + lax.rem(i * 7, 15) + 1, 16)

    def along_y(i):
        for d in (1, 3, 2):
            to = lax.rem(y + d, 4)
            pltpu.make_async_remote_copy(
                src_ref=block(to, target(i)), dst_ref=stage.at[d - 1, i], send_sem=y_send, recv_sem=y_recv.at[d - 1, i],
                device_id=dev(g, to, zc), device_id_type=MESH).start()

    def along_z(src, slot, i, which):
        pltpu.make_async_remote_copy(
            src_ref=src, dst_ref=buf.at[slot], send_sem=z_send, recv_sem=z_recv.at[which],
            device_id=dev(g, y, target(i)), device_id_type=MESH).start()

    def forward(d, i, which):
        pltpu.make_async_copy(stage.at[0, 0], stage.at[d - 1, i], y_recv.at[d - 1, i]).wait()
        along_z(stage.at[d - 1, i], lax.rem(y - d + 4, 4) * 16 + zc, i, which)

    def own(i, which):
        along_z(block(y, target(i)), r, i, which)

    def own_column():
        for d in (1, 3, 2):
            to = lax.rem(y + d, 4)
            pltpu.make_async_remote_copy(
                src_ref=block(to, zc), dst_ref=buf.at[r], send_sem=y_send, recv_sem=z_recv.at[phase_of],
                device_id=dev(g, to, zc), device_id_type=MESH).start()
        pltpu.make_async_copy(block(y, zc), buf.at[r], z_recv.at[phase_of]).start()

    @pl.when(y < 2)
    def _():
        other = jnp.where(y == 0, 3, 1)

        @pl.loop(0, LAG)
        def _(i):
            along_y(i)
            own(i, 0)

        @pl.loop(LAG, 15)
        def _(i):
            along_y(i)
            own(i, 0)
            forward(other, i - LAG, 0)

        own_column()

        @pl.loop(15 - LAG, 15)
        def _(i):
            forward(other, i, 0)

    @pl.when(y >= 2)
    def _():
        @pl.loop(0, FILL)
        def _(i):
            along_y(i)
            own(i, phase_of)

        @pl.loop(0, 15)
        def _(i):
            forward(y, i, 0)
            forward(y - 1, i, 0)

            @pl.when(i + FILL < 15)
            def _():
                along_y(i + FILL)

        own_column()

    def send_plane(src, lo, hi):
        d = lax.rem(y - src + 4, 4)

        @pl.when(d != 0)
        def _():
            @pl.loop(lo, hi)
            def _(i):
                forward(d, i, src - 1)

        if hi > FILL:
            @pl.when(d == 0)
            def _():
                @pl.loop(lo, hi)
                def _(i):
                    own(i, src - 1)

    def wait(ref, sem):
        pltpu.make_async_copy(ref, ref, sem).wait()

    def weighted(lo, n, pair):
        v = buf[lo // 4:(lo + n) // 4, pl.ds(pl.multiple_of(pair * 8, 8), 8), :].reshape(n // 8, 2, 8, 128)
        even, odd = v[:, 0], v[:, 1]
        low = lax.broadcasted_iota(jnp.int32, even.shape, 1) < 4
        left = jnp.where(low, even, pltpu.roll(odd, 4, 1)).reshape(n, 128)
        right = jnp.where(low, pltpu.roll(even, 4, 1), odd).reshape(n, 128)
        cols = pl.ds(pl.multiple_of(pair * 256, 256), 256)
        for k, v in enumerate(split3(jnp.concatenate([left, right], axis=1) * jnp.sqrt(w_ref[:, cols]))):
            xs[k, lo:lo + n, cols] = v

    def rows_gram(lo, n):
        end = lo + n
        gram[:3 * n, :end] = jnp.zeros((3 * n, end), F32)

        @pl.loop(0, 4)
        def _(quad):
            for p in range(4):
                weighted(lo, n, quad * 4 + p)
            cols = pl.ds(pl.multiple_of(quad * 1024, 1024), 1024)
            h, m, l = xs[0, lo:end, cols], xs[1, lo:end, cols], xs[2, lo:end, cols]
            gram[:3 * n, :end] += mm(jnp.concatenate([h, m, l], axis=0), xs[0, :end, cols], NT)
            gram[:2 * n, :end] += mm(jnp.concatenate([h, m], axis=0), xs[1, :end, cols], NT)
            gram[:n, :end] += mm(h, xs[2, :end, cols], NT)

        return (gram[2 * n:3 * n, :end] + gram[n:2 * n, :end]) + gram[:n, :end]

    def send(src, dst, i, to):
        pltpu.make_async_remote_copy(src_ref=src, dst_ref=dst, send_sem=red_send.at[i], recv_sem=red_recv.at[i],
                                     device_id=to, device_id_type=MESH).start()

    def part(ref, k, px, py):
        return ref.at[k, pl.ds(pl.multiple_of((px * 4 + py) * 8, 8), 8)]

    def sum_start(k):
        for dx, dy in plane:
            px, py = lax.rem(g + dx, 4), lax.rem(y + dy, 4)
            send(part(pack, k, px, py), parts.at[k, dx * 4 + dy - 1], 3 * k, dev(px, py, zc))

    def sum_second(k):
        wait(parts.at[k], red_recv.at[3 * k])
        mine = part(pack, k, g, y)[...]
        for i in range(15):
            mine = mine + parts[k, i]
        zparts[k, zc] = mine

        @pl.loop(0, 15)
        def _(i):
            send(zparts.at[k, zc], zparts.at[k, zc], 3 * k + 1, dev(g, y, target(i)))

    def sum_third(k):
        wait(zparts.at[k, pl.ds(0, 15)], red_recv.at[3 * k + 1])
        total = zparts[k, 0]
        for i in range(1, 16):
            total = total + zparts[k, i]
        here = part(res, k, g, y)
        here[...] = total * SCALE
        for dx, dy in plane:
            send(here, here, 3 * k + 2, dev(lax.rem(g + dx, 4), lax.rem(y + dy, 4), zc))

    def sum_done(k):
        wait(parts.at[k], red_recv.at[3 * k + 2])

    def reduce_end(k):
        wait(parts.at[k], red_send.at[3 * k])
        wait(parts.at[k], red_send.at[3 * k + 1])
        wait(parts.at[k], red_send.at[3 * k + 2])

    def factor_rows(lo, strip, corner):
        hi = lo + B
        above = p_ref[:lo, :lo]
        side = dot(strip, above, NT)
        both = eliminate(corner - dot(side, side, NT))
        inv = both[:, B:]
        tri_ref[lo:hi, lo:hi] = keep_upper(both[:, :B])
        tri_ref[:lo, lo:hi] = dot(above, strip, NT)
        p_ref[lo:hi, :lo] = -dot(inv, dot(side, above, NN), NN)
        p_ref[lo:hi, lo:hi] = inv

    def project(w3, lo, n, q):
        end = lo + n
        wh, wm, wl = w3
        w_hml = jnp.concatenate([wh, wm, wl], axis=0)
        w_hm = jnp.concatenate([wh, wm], axis=0)
        for i in range(4):
            cols = pl.ds(q * 1024 + i * 256, 256)
            s = mm(w_hml, xs[0, :end, cols], NN)
            t = mm(w_hm, xs[1, :end, cols], NN)
            u = mm(wh, xs[2, :end, cols], NN)
            tmp[:n, i * 256:i * 256 + 256] = (s[2 * n:] + t[n:] + u) + (s[n:2 * n] + t[:n]) + s[:n]
        v = [tmp[:n, k * 128:k * 128 + 128].reshape(n // 8, 8, 128) for k in range(8)]
        sub = lax.broadcasted_iota(jnp.int32, (n // 8, 8, 128), 1)
        for step in (4, 2, 1):
            keep = (sub & step) == 0
            for k in range(8):
                if k & step == 0:
                    a, b = v[k], v[k + step]
                    v[k] = jnp.where(keep, a, pltpu.roll(b, step, 1))
                    v[k + step] = jnp.where(keep, pltpu.roll(a, 8 - step, 1), b)
        for s in range(8):
            out_ref[lo // 8:end // 8, s, 8 * q:8 * q + 8, :] = v[s]

    p_ref[...] = jnp.zeros_like(p_ref)
    tri_ref[...] = jnp.zeros_like(tri_ref)
    send_plane(2, 0, FILL)
    send_plane(2, FILL, 15)

    wait(buf.at[pl.ds(0, 32)], z_recv.at[0])
    pack[0] = rows_gram(0, 128)
    sum_start(0)
    send_plane(3, 0, FILL)
    send_plane(3, FILL, HELD)

    wait(buf.at[pl.ds(32, 16)], z_recv.at[1])
    strip = rows_gram(128, B)
    pack[1, :B] = strip[:, :128]
    pack[1, B:, :B] = strip[:, 128:]
    pack[1, B:, B:] = jnp.zeros((B, B), F32)
    sum_second(0)
    sum_start(1)
    send_plane(3, HELD, 15)
    sum_third(0)
    sum_second(1)

    wait(buf.at[pl.ds(48, 16)], z_recv.at[2])
    strip = rows_gram(192, B)
    pack[2, :B] = strip[:, :128]
    pack[2, B:] = strip[:, 128:]
    sum_start(2)
    sum_third(1)
    sum_done(0)
    both = eliminate(res[0, :B, :B])
    p_ref[:B, :B] = both[:, B:]
    tri_ref[:B, :B] = keep_upper(both[:, :B])
    sum_second(2)
    factor_rows(B, res[0, B:, :B], res[0, B:, B:])
    sum_third(2)
    sum_done(1)
    factor_rows(128, res[1, :B], res[1, B:, :B])
    w3 = split3(p_ref[:192, :192])
    for q in range(4):
        project(w3, 0, 192, q)
    sum_done(2)
    factor_rows(192, jnp.concatenate([res[2, :B], res[2, B:, :B]], axis=1), res[2, B:, B:])
    w3 = split3(p_ref[192:, :])
    for q in range(4):
        project(w3, 192, B, q)

    for k in range(3):
        reduce_end(k)
    wait(buf.at[pl.ds(0, 48)], y_send)
    wait(buf.at[pl.ds(0, 60)], z_send)


def store_kernel(modes_ref, upper_ref, out_ref, tri_ref, sems):
    one = pltpu.make_async_copy(modes_ref, out_ref, sems.at[0])
    two = pltpu.make_async_copy(upper_ref, tri_ref, sems.at[1])
    one.start()
    two.start()
    one.wait()
    two.wait()


def body(snapshots, lumped_mass):
    x = snapshots.reshape(4, 2048, 128).transpose(1, 0, 2).reshape(8192, 128)
    anywhere = pl.BlockSpec(memory_space=pl.ANY)
    vmem = pl.BlockSpec(memory_space=pltpu.VMEM)
    dma = pltpu.SemaphoreType.DMA

    def room(*shape):
        return pltpu.VMEM(shape, F32)

    modes, upper = pl.pallas_call(
        pod_kernel,
        name="pod",
        out_shape=(jax.ShapeDtypeStruct((32, 8, TILES, 128), F32), jax.ShapeDtypeStruct((K, K), F32)),
        in_specs=[anywhere, vmem],
        out_specs=(vmem, vmem),
        scratch_shapes=[
            room(64, 128, 128), room(3, 15, 128, 128), pltpu.VMEM((3, K, COORDS), BF16),
            room(384, K), room(K, K), room(192, 1024),
            room(3, 128, 128), room(3, 15, 8, 128), room(3, 16, 8, 128), room(3, 128, 128),
            dma, dma((3, 15)), dma, dma((3,)), dma((9,)), dma((9,)),
        ],
        compiler_params=pltpu.CompilerParams(collective_id=0, has_side_effects=True, vmem_limit_bytes=VMEM_LIMIT),
    )(x, lumped_mass)
    out, tri = pl.pallas_call(
        store_kernel,
        name="store",
        out_shape=(jax.ShapeDtypeStruct(modes.shape, F32), jax.ShapeDtypeStruct((K, K), F32)),
        in_specs=[anywhere, anywhere],
        out_specs=(anywhere, anywhere),
        scratch_shapes=[dma((2,))],
        compiler_params=pltpu.CompilerParams(vmem_limit_bytes=STORE_LIMIT),
    )(modes, upper)
    return out.reshape(K, 1, COORDS), tri


STORE_LIMIT = 40 * 2**20
VMEM_LIMIT = 47 * 2**20


def solution(mesh):
    return jax.shard_map(
        body,
        mesh=mesh,
        in_specs=(P("row", "grp"), P("grp", "row")),
        out_specs=(P(None, "grp", "row"), P()),
        check_vma=False,
    )
```

time: 466 us -> 139 us (0.30)
  waiting for transfers between devices: 331 us -> 0 us
  Pallas kernels: 0 us -> 137 us
  other arithmetic: 65.9 us -> 0 us
  local copies, waits for them, and re-layouts: 23 us -> 0.71 us
  matrix products: 15.7 us -> 0 us
  between operations: 15.5 us -> 0.65 us
  starting transfers between devices: 13.4 us -> 0 us
    psum x1 -> x0, waiting for transfers between devices: 235 us -> none  [body(): full_gram = lax.psum(own_gram, ('row', 'grp'))]
    pallas_call x0 -> x2, Pallas kernels: none -> 137 us  [the longest x1 135 us: body(): pl.pallas_call(pod_kernel, name='pod', out_shape=(jax.ShapeDtypeStruct((3...]
    all_to_all x1 -> x0, waiting for transfers between devices: 95.8 us -> none  [body(): lax.all_to_all(snapshots, 'row', split_axis=1, concat_axis=0, tiled=True)]
    another operation x8 -> x0, other arithmetic: 53.9 us -> none  [the longest x6 34 us: body(): factor_low = jnp.linalg.cholesky(full_gram)]
    all_to_all x1 -> x0, starting transfers between devices: 13.4 us -> none  [body(): lax.all_to_all(snapshots, 'row', split_axis=1, concat_axis=0, tiled=True)]
    mul x2 -> x0, other arithmetic: 10.5 us -> none  [body(): weighted = received * jnp.sqrt(lumped_mass)]
    another operation x5 -> x0, matrix products: 7.98 us -> none  [the longest x3 7.51 us: body(): jax.scipy.linalg.solve_triangular(factor_low, weighted, lower=True)]
    dot_general x1 -> x0, matrix products: 7.69 us -> none  [body(): lax.dot_general(weighted, weighted, (((1,), (1,)), ((), ())), precision=l...]
  transfers between devices with their start and end apart: 2 -> 0, of which waited for: 2 -> 0; matrix products, arithmetic and copies ran while one was open for 1% -> 0% of each run, Pallas kernels for 0% -> 0%
where the time goes in v2:
time: 139 us
  Pallas kernels  137 us (99%)
    pallas_call x1, Pallas kernels, body(): pl.pallas_call(pod_kernel, name='pod', out_shape=(jax.ShapeDtypeStruct((3...  135 us

profile of v2, /device:TPU:1, one launch (start us, length us, event | category | flops | bytes accessed | tf_op | source)
XLA Modules:
  0.0 138.7 jit_solution(4501412550474492197)
XLA Ops:
  0.6 0.0 copy-start
  0.6 0.7 copy-done
  1.3 135.3 %pod.1 = (f32[32,8,32,128]{3,2,1,0:T(8,128)S(1)}, f32[256,256]{1,0:T(8,128)S(1)}) custom-call(f32[8192,128]{1,0:T(8,128)} %bitcast.6, f32[1,4096]{1,0:T(1,128)S(1)} %copy-done), custom_call_target="tpu_custom_call" | custom-call | tf_op jit(solution)/shard_map/pod/pallas_call | solution.py:365
  136.6 2.1 %store.1 = (f32[32,8,32,128]{3,2,1,0:T(8,128)}, f32[256,256]{1,0:T(8,128)}) custom-call(f32[32,8,32,128]{3,2,1,0:T(8,128)S(1)} %get-tuple-element.6.modes_ref, f32[256,256]{1,0:T(8,128)S(1)} %get-tuple-element.7.upper_ref), custom_call_target="tpu_custom_call" | custom-call | tf_op jit(solution)/shard_map/store/pallas_call | solution.py:379
Async XLA Ops:
  0.6 0.7 copy-start

commit v3 on v2

--- a/solution.py
+++ b/solution.py
@@ -11,8 +11,8 @@
 K = 256
 COORDS = 4096
 TILES = 32
-FILL = 3
-HELD = 8
+FILL = 6
+HELD = 9
 LAG = 5
 B = 64
 STEP = 8
@@ -324,11 +324,11 @@
     both = eliminate(res[0, :B, :B])
     p_ref[:B, :B] = both[:, B:]
     tri_ref[:B, :B] = keep_upper(both[:, :B])
+    factor_rows(B, res[0, B:, :B], res[0, B:, B:])
     sum_second(2)
-    factor_rows(B, res[0, B:, :B], res[0, B:, B:])
-    sum_third(2)
     sum_done(1)
     factor_rows(128, res[1, :B], res[1, B:, :B])
+    sum_third(2)
     w3 = split3(p_ref[:192, :192])
     for q in range(4):
         project(w3, 0, 192, q)

time: 139 us -> 137 us (0.986)
  Pallas kernels: 137 us -> 135 us
    pallas_call x1, Pallas kernels: 135 us -> 133 us  [body(): pl.pallas_call(pod_kernel, name='pod', out_shape=(jax.ShapeDtypeStruct((3...]
where the time goes in v3:
time: 137 us; the launch traced here: 136 us
  Pallas kernels  135 us (99%)
    pallas_call x1, Pallas kernels, body(): pl.pallas_call(pod_kernel, name='pod', out_shape=(jax.ShapeDtypeStruct((3...  133 us

profile of v3, /device:TPU:1, one launch (start us, length us, event | category | flops | bytes accessed | tf_op | source)
XLA Modules:
  0.0 136.5 jit_solution(9293717940554297384)
XLA Ops:
  0.6 0.0 copy-start
  0.6 0.7 copy-done
  1.3 133.0 %pod.1 = (f32[32,8,32,128]{3,2,1,0:T(8,128)S(1)}, f32[256,256]{1,0:T(8,128)S(1)}) custom-call(f32[8192,128]{1,0:T(8,128)} %bitcast.6, f32[1,4096]{1,0:T(1,128)S(1)} %copy-done), custom_call_target="tpu_custom_call" | custom-call | tf_op jit(solution)/shard_map/pod/pallas_call | solution.py:365
  134.4 2.1 %store.1 = (f32[32,8,32,128]{3,2,1,0:T(8,128)}, f32[256,256]{1,0:T(8,128)}) custom-call(f32[32,8,32,128]{3,2,1,0:T(8,128)S(1)} %get-tuple-element.6.modes_ref, f32[256,256]{1,0:T(8,128)S(1)} %get-tuple-element.7.upper_ref), custom_call_target="tpu_custom_call" | custom-call | tf_op jit(solution)/shard_map/store/pallas_call | solution.py:379
Async XLA Ops:
  0.6 0.7 copy-start

commit v4 on v3

--- a/solution.py
+++ b/solution.py
@@ -11,8 +11,8 @@
 K = 256
 COORDS = 4096
 TILES = 32
-FILL = 6
-HELD = 9
+FILL = 9
+HELD = 12
 LAG = 5
 B = 64
 STEP = 8

time: 137 us -> 135 us (0.985)
  Pallas kernels: 135 us -> 133 us
    pallas_call x1, Pallas kernels: 133 us -> 131 us  [body(): pl.pallas_call(pod_kernel, name='pod', out_shape=(jax.ShapeDtypeStruct((3...]
where the time goes in v4:
time: 135 us
  Pallas kernels  133 us (99%)
    pallas_call x1, Pallas kernels, body(): pl.pallas_call(pod_kernel, name='pod', out_shape=(jax.ShapeDtypeStruct((3...  131 us

profile of v4, /device:TPU:1, one launch (start us, length us, event | category | flops | bytes accessed | tf_op | source)
XLA Modules:
  0.0 134.6 jit_solution(18163486435816885701)
XLA Ops:
  0.6 0.0 copy-start
  0.6 0.7 copy-done
  1.3 131.1 %pod.1 = (f32[32,8,32,128]{3,2,1,0:T(8,128)S(1)}, f32[256,256]{1,0:T(8,128)S(1)}) custom-call(f32[8192,128]{1,0:T(8,128)} %bitcast.6, f32[1,4096]{1,0:T(1,128)S(1)} %copy-done), custom_call_target="tpu_custom_call" | custom-call | tf_op jit(solution)/shard_map/pod/pallas_call | solution.py:365
  132.5 2.1 %store.1 = (f32[32,8,32,128]{3,2,1,0:T(8,128)}, f32[256,256]{1,0:T(8,128)}) custom-call(f32[32,8,32,128]{3,2,1,0:T(8,128)S(1)} %get-tuple-element.6.modes_ref, f32[256,256]{1,0:T(8,128)S(1)} %get-tuple-element.7.upper_ref), custom_call_target="tpu_custom_call" | custom-call | tf_op jit(solution)/shard_map/store/pallas_call | solution.py:379
Async XLA Ops:
  0.6 0.7 copy-start

commit v5 on v4

--- a/solution.py
+++ b/solution.py
@@ -11,8 +11,8 @@
 K = 256
 COORDS = 4096
 TILES = 32
-FILL = 9
-HELD = 12
+FILL = 12
+HELD = 14
 LAG = 5
 B = 64
 STEP = 8

time: 135 us -> 136 us (level)
  Pallas kernels: 133 us -> 135 us
    pallas_call x1, Pallas kernels: 131 us -> 133 us  [body(): pl.pallas_call(pod_kernel, name='pod', out_shape=(jax.ShapeDtypeStruct((3...]
where the time goes in v5:
time: 136 us
  Pallas kernels  135 us (99%)
    pallas_call x1, Pallas kernels, body(): pl.pallas_call(pod_kernel, name='pod', out_shape=(jax.ShapeDtypeStruct((3...  133 us

profile of v5, /device:TPU:1, one launch (start us, length us, event | category | flops | bytes accessed | tf_op | source)
XLA Modules:
  0.0 136.3 jit_solution(1538007608865841045)
XLA Ops:
  0.6 0.0 copy-start
  0.6 0.7 copy-done
  1.3 132.8 %pod.1 = (f32[32,8,32,128]{3,2,1,0:T(8,128)S(1)}, f32[256,256]{1,0:T(8,128)S(1)}) custom-call(f32[8192,128]{1,0:T(8,128)} %bitcast.6, f32[1,4096]{1,0:T(1,128)S(1)} %copy-done), custom_call_target="tpu_custom_call" | custom-call | tf_op jit(solution)/shard_map/pod/pallas_call | solution.py:365
  134.2 2.1 %store.1 = (f32[32,8,32,128]{3,2,1,0:T(8,128)}, f32[256,256]{1,0:T(8,128)}) custom-call(f32[32,8,32,128]{3,2,1,0:T(8,128)S(1)} %get-tuple-element.6.modes_ref, f32[256,256]{1,0:T(8,128)S(1)} %get-tuple-element.7.upper_ref), custom_call_target="tpu_custom_call" | custom-call | tf_op jit(solution)/shard_map/store/pallas_call | solution.py:379
Async XLA Ops:
  0.6 0.7 copy-start
